TPU v7x, 256 devices: a whole 4x4x8 slice. The times are simulated.
256 devices in a mesh: row: 16 (over y, x_hi, core), col: 8 (over z), depth: 2 (over x_lo).
Axes of the slice: x: 4 (x_hi: 2, x_lo: 2; x = x_hi * 2 + x_lo), y: 4, z: 8, core: 2. Of those that a mesh axis runs over, the one named last changes fastest.
Arguments:
- covariance: float32 [7168, 7168], P('row', 'col'), may hold values from -1 to 5, as said below
- iterate: float32 [7168, 7168], P('row', 'col'), may hold values from -1 to 1.5
Outputs:
- refreshed: float32 [7168, 4096], P(('row', 'depth'), 'col')
Inputs may be any that keep to these rules, and one draw needn't show every extreme that they name: `covariance`: symmetric.
All inputs are finite; a program needn't handle non-finite values.
Results may differ from a plain program's by a relative error of at most 0.00008.
Values sent between devices are 32-bit elements; how exact they have to be, the bound alone decides.
No kernel may reach another device: no remote copies, remote signals or barrier semaphores. Data moves between devices by JAX's collectives and lax.ppermute only.
A program may use at most 64 MiB of HBM per device.

v0:
```python
import jax
import jax.numpy as jnp
from jax import lax
from jax.sharding import PartitionSpec as P

PERIOD = 896
SLAB = 512


def contraction_half(matrix, depth_pos, half_rows):
    tile_rows = matrix.shape[0]
    blocks = matrix.shape[1] // (2 * half_rows)
    shaped = matrix.reshape(tile_rows, blocks, 2, half_rows)
    picked = lax.dynamic_index_in_dim(shaped, depth_pos, 2, keepdims=False)
    return picked.reshape(tile_rows, blocks * half_rows)


def local(covariance, iterate):
    tile_rows = covariance.shape[0]
    tile_cols = covariance.shape[1]
    half_rows = tile_rows // 2
    depth_pos = lax.axis_index("depth")
    periods = tile_cols // PERIOD
    slab_width = periods * SLAB
    high = lax.Precision.HIGHEST
    slab_tile = iterate.reshape(tile_rows, periods, PERIOD)[:, :, :SLAB].reshape(
        tile_rows, slab_width
    )
    slab_half = lax.dynamic_slice_in_dim(slab_tile, depth_pos * half_rows, half_rows, 0)
    cov_half = contraction_half(covariance, depth_pos, half_rows)
    iter_half = contraction_half(iterate, depth_pos, half_rows)
    slab_whole = lax.all_gather(slab_half, "row", axis=0, tiled=True)
    rows_part = slab_whole
    partial_product = jnp.dot(
        lax.all_gather(cov_half, "col", axis=1, tiled=True),
        rows_part,
        precision=high,
        preferred_element_type=jnp.float32,
    )
    full_product = lax.psum(partial_product, "depth")
    product_share = lax.dynamic_slice_in_dim(full_product, depth_pos * half_rows, half_rows, 0)
    row_ids = (
        lax.axis_index("row") * tile_rows
        + depth_pos * half_rows
        + jnp.arange(half_rows, dtype=jnp.int32)
    )
    offsets = jnp.arange(slab_width, dtype=jnp.int32)
    col_ids = lax.axis_index("col") * tile_cols + offsets // SLAB * PERIOD + offsets % SLAB
    select = (row_ids[:, None] == col_ids[None, :]).astype(jnp.float32)
    residual_share = 2.0 * select - product_share
    residual_whole = lax.all_gather(residual_share, "row", axis=0, tiled=True)
    rows_part = residual_whole
    partial_result = jnp.dot(
        lax.all_gather(iter_half, "col", axis=1, tiled=True),
        rows_part,
        precision=high,
        preferred_element_type=jnp.float32,
    )
    return lax.psum_scatter(partial_result, "depth", scatter_dimension=0, tiled=True)


def solution(mesh):
    in_specs = (P("row", "col"), P("row", "col"))
    out_specs = P(("row", "depth"), "col")
    return jax.shard_map(local, mesh=mesh, in_specs=in_specs, out_specs=out_specs, check_vma=False)
```

profile of v0, /device:TPU:16, one launch (start us, length us, event | category | flops | bytes accessed | tf_op | source)
XLA Modules:
  0.0 451.6 jit_solution(15063966996268585952)
XLA Ops:
  6.5 4.4 reshape.48
  11.0 1.7 constant_dynamic-slice_fusion.1
  12.7 3.6 copy.6
  16.3 0.0 all-gather.8.cloned.1.call-update
  16.3 0.0 all-gather.12.cloned.1.call-start
  16.3 0.1 slice.4
  16.5 0.8 constant_dynamic-slice_fusion
  17.3 0.0 all-gather.12.cloned.1.call-update
  17.3 0.0 all-reduce.2.cloned.1.call-start
  17.3 86.2 %all-gather.8.cloned.1.call-done = f32[448,3584]{0,1:T(8,128)} async-done(((f32[448,448]{0,1:T(8,128)}), f32[448,3584]{0,1:T(8,128)}) %all-gather.8.cloned.1.call-update) | async-done | bytes 6422544 | tf_op jit(solution)/shard_map/all_gather | solution.py:35
  103.5 73.4 %all-gather.12.cloned.1.call-done = f32[3584,1,512]{2,0,1:T(8,128)} async-done(((f32[224,1,512]{2,0,1:T(8,128)}), f32[3584,1,512]{2,0,1:T(8,128)}) %all-gather.12.cloned.1.call-update) | async-done | bytes 7340048 | tf_op jit(solution)/shard_map/all_gather | solution.py:32
  176.9 17.5 %fusion = f32[448,512]{1,0:T(8,128)} fusion(f32[448,3584]{0,1:T(8,128)} %all-gather.8.cloned.1.call-done, f32[3584,1,512]{2,0,1:T(8,128)} %all-gather.12.cloned.1.call-done), kind=kOutput, calls=%fused_computation | convolution fusion | flops 9865003008 | bytes 14680064 | tf_op jit(solution)/shard_map/dot_general | solution.py:34
  194.4 0.2 all-gather.6.cloned.1.call-start
  194.6 2.8 reshape.46
  197.4 0.8 constant_dynamic-slice_fusion.2
  198.2 2.2 copy.5
  200.4 0.0 all-gather.10.cloned.1.call-start
  200.5 42.4 %all-reduce.2.cloned.1.call-done = f32[448,512]{1,0:T(8,128)} async-done(((f32[448,512]{1,0:T(8,128)}), f32[448,512]{1,0:T(8,128)}) %all-reduce.2.cloned.1.call-update) | async-done | bytes 917520 | tf_op jit(solution)/shard_map/psum | solution.py:40
  242.9 1.9 dynamic-slice_subtract_fusion
  244.8 0.0 reduce-scatter.2.cloned.1.call-start
  244.9 85.1 %all-gather.6.cloned.1.call-done = f32[448,3584]{0,1:T(8,128)} async-done(((f32[448,448]{0,1:T(8,128)}), f32[448,3584]{0,1:T(8,128)}) %all-gather.6.cloned.1.call-update) | async-done | bytes 6422544 | tf_op jit(solution)/shard_map/all_gather | solution.py:54
  330.0 73.6 %all-gather.10.cloned.1.call-done = f32[3584,512]{1,0:T(8,128)} async-done(((f32[224,512]{1,0:T(8,128)}), f32[3584,512]{1,0:T(8,128)}) %all-gather.10.cloned.1.call-update) | async-done | bytes 7340048 | tf_op jit(solution)/shard_map/all_gather | solution.py:51
  403.6 17.5 %fusion.12 = f32[448,512]{1,0:T(8,128)} fusion(f32[448,3584]{0,1:T(8,128)} %all-gather.6.cloned.1.call-done, f32[3584,512]{1,0:T(8,128)} %all-gather.10.cloned.1.call-done), kind=kOutput, calls=%fused_computation.21 | convolution fusion | flops 9865003008 | bytes 14680064 | tf_op jit(solution)/shard_map/dot_general | solution.py:53
  421.1 23.6 %reduce-scatter.2.cloned.1.call-done = f32[224,512]{1,0:T(8,128)} async-done(((f32[448,512]{1,0:T(8,128)}), f32[224,512]{1,0:T(8,128)}) %reduce-scatter.2.cloned.1.call-update) | async-done | bytes 458768 | tf_op jit(solution)/shard_map/reduce_scatter | solution.py:59
  (9 shorter events, 0.1 us)
Async XLA Ops:
  6.5 9.8 %copy-start = (f32[448,896]{1,0:T(8,128)S(1)}, f32[448,896]{1,0:T(8,128)}, u32[]{:S(2)}) copy-start(f32[448,896]{1,0:T(8,128)} %param.3) | copy-start | bytes 4816900
  6.5 97.0 %all-gather.8.cloned.1.call-start = ((), (), s32[]{:S(2)}) async-start(), calls=%async_computation.2 | async-start | bytes 8257536 | tf_op jit(solution)/shard_map/all_gather | solution.py:35
  16.3 160.6 %all-gather.12.cloned.1.call-start = ((), (), s32[]{:S(2)}) async-start(), calls=%async_computation.6 | async-start | bytes 7798784 | tf_op jit(solution)/shard_map/all_gather | solution.py:32
  17.3 225.6 %all-reduce.2.cloned.1.call-start = ((), (), s32[]{:S(2)}) async-start(), calls=%async_computation.3 | async-start | bytes 1835008 | tf_op jit(solution)/shard_map/psum | solution.py:40
  194.4 135.6 %all-gather.6.cloned.1.call-start = ((), (), s32[]{:S(2)}) async-start(), calls=%async_computation.1 | async-start | bytes 8257536 | tf_op jit(solution)/shard_map/all_gather | solution.py:54
  200.4 203.2 %all-gather.10.cloned.1.call-start = ((), (), s32[]{:S(2)}) async-start(), calls=%async_computation.4 | async-start | bytes 7798784 | tf_op jit(solution)/shard_map/all_gather | solution.py:51
  244.8 199.9 %reduce-scatter.2.cloned.1.call-start = ((), (), s32[]{:S(2)}) async-start(), calls=%async_computation.5 | async-start | bytes 1376256 | tf_op jit(solution)/shard_map/reduce_scatter | solution.py:59
Sparse Core Ops, SparseCore 0:
  16.4 87.0 all-gather.7
  106.3 70.5 all-gather.11
  194.5 48.3 all-reduce.1
  244.7 85.2 all-gather.5
  333.0 70.5 all-gather.9
  421.3 23.4 reduce-scatter.1
where the time goes:
time: 453 us; the launch traced here: 452 us
  waiting for transfers between devices  384 us (85%)
  matrix products  35 us (8%)
  local copies, waits for them, and re-layouts  16.4 us (4%)
  between operations  13.5 us (3%)
    all_gather x1, waiting for transfers between devices, local(): lax.all_gather(cov_half, 'col', axis=1, tiled=True)  86.2 us
    all_gather x1, waiting for transfers between devices, local(): lax.all_gather(iter_half, 'col', axis=1, tiled=True)  85.1 us
    all_gather x1, waiting for transfers between devices, local(): residual_whole = lax.all_gather(residual_share, 'row', axis=0, tiled=True)  73.6 us
    all_gather x1, waiting for transfers between devices, local(): slab_whole = lax.all_gather(slab_half, 'row', axis=0, tiled=True)  73.4 us
    psum x1, waiting for transfers between devices, local(): full_product = lax.psum(partial_product, 'depth')  42.4 us
    reduce_scatter x1, waiting for transfers between devices, local(): lax.psum_scatter(partial_result, 'depth', scatter_dimension=0, tiled=True)  23.6 us
    dot_general x1, matrix products, local(): jnp.dot(lax.all_gather(cov_half, 'col', axis=1, tiled=True), rows_part, p...  17.5 us
    dot_general x1, matrix products, local(): jnp.dot(lax.all_gather(iter_half, 'col', axis=1, tiled=True), rows_part,...  17.5 us
  transfers between devices with their start and end apart: 6, of which 6 were waited for; matrix products, arithmetic and copies ran while one was open for 2% of the time, Pallas kernels for 0%

commit v1 on v0

v1 whole, which is shorter than its diff:
```python
import functools
import jax
import jax.numpy as jnp
from jax import lax
from jax.experimental import pallas as pl
from jax.experimental.pallas import tpu as pltpu
from jax.sharding import PartitionSpec as P

PERIOD = 896
SLAB = 512
F32 = jnp.float32
BF16 = jnp.bfloat16
VMEM_LIMIT = 48 * 1024 * 1024


def split(value):
    hi = value.astype(BF16)
    lo = (value - hi.astype(F32)).astype(BF16)
    return hi, lo


def dot3(a_hi, a_lo, b_hi, b_lo):
    dot = functools.partial(jnp.dot, preferred_element_type=F32)
    return dot(a_hi, b_hi) + (dot(a_hi, b_lo) + dot(a_lo, b_hi))


def lower_lanes(shape):
    return lax.broadcasted_iota(jnp.int32, shape, len(shape) - 1) < 64


def swap(value):
    return pltpu.roll(value, 64, axis=value.ndim - 1)


def row_offset(scal, block):
    half, part, first, second = block // 8, block // 4 % 2, block // 2 % 2, block % 2
    core, b1, b2 = scal[0], scal[3], scal[4]
    half = core if half else 1 - core
    b1_first, b2_first = (b1, b2) if part == 0 else (b2, b1)
    first = b1_first if first else 1 - b1_first
    second = b2_first if second else 1 - b2_first
    return pl.multiple_of(half * 448 + part * 224 + first * 112 + second * 56, 8)


def transpose_kernel(scal, tile, hi, lo, turned, ordered):
    turned[...] = tile[...].T
    for block in range(16):
        ordered[block * 56 : block * 56 + 56] = turned[pl.ds(row_offset(scal, block), 56)]
    hi[...], lo[...] = split(ordered[...])


def transposed(scal, tile):
    rows, cols = tile.shape
    return pl.pallas_call(
        transpose_kernel,
        grid_spec=pltpu.PrefetchScalarGridSpec(
            num_scalar_prefetch=1,
            grid=(1,),
            in_specs=[pl.BlockSpec((rows, cols), lambda i, s: (0, 0))],
            out_specs=[pl.BlockSpec((cols, rows), lambda i, s: (0, 0))] * 2,
            scratch_shapes=[pltpu.VMEM((cols, rows), F32)] * 2,
        ),
        out_shape=[jax.ShapeDtypeStruct((cols, rows), BF16)] * 2,
        compiler_params=pltpu.CompilerParams(vmem_limit_bytes=VMEM_LIMIT),
        cost_estimate=pl.CostEstimate(flops=0, bytes_accessed=8 * rows * cols, transcendentals=0),
        name="transpose_split",
    )(scal, tile)


def first_kernel(gathered, own_hi, own_lo, par_hi, par_lo, send, keep, w_hi, w_lo):
    step = pl.program_id(0)

    @pl.when(step == 0)
    def _():
        lower = lower_lanes((448, 128))
        for pair in range(4):
            even, odd = gathered[2 * pair], gathered[2 * pair + 1]
            cols = slice(pair * 128, pair * 128 + 128)
            own = jnp.where(lower, even, swap(odd))
            par = jnp.where(lower, swap(even), odd)
            w_hi[:448, cols], w_lo[:448, cols] = split(own)
            w_hi[448:, cols], w_lo[448:, cols] = split(par)

    total = dot3(own_hi[...], own_lo[...], w_hi[:448], w_lo[:448])
    total += dot3(par_hi[...], par_lo[...], w_hi[448:], w_lo[448:])

    @pl.when(step < 2)
    def _():
        send[...] = total

    @pl.when(step >= 2)
    def _():
        keep[...] = total


def first_product(gathered, own, par):
    tile = pl.BlockSpec((224, 448), lambda m: (m, 0))
    return pl.pallas_call(
        first_kernel,
        grid=(4,),
        in_specs=[pl.BlockSpec((8, 448, 128), lambda m: (0, 0, 0))] + [tile] * 4,
        out_specs=[
            pl.BlockSpec((224, 512), lambda m: (jnp.minimum(m, 1), 0)),
            pl.BlockSpec((224, 512), lambda m: (jnp.maximum(m - 2, 0), 0)),
        ],
        scratch_shapes=[pltpu.VMEM((896, 512), BF16)] * 2,
        out_shape=[jax.ShapeDtypeStruct((448, 512), F32)] * 2,
        compiler_params=pltpu.CompilerParams(vmem_limit_bytes=VMEM_LIMIT),
        cost_estimate=pl.CostEstimate(
            flops=6 * 896 * 896 * 512, bytes_accessed=7 << 20, transcendentals=0
        ),
        name="first_product",
    )(gathered, *own, *par)


def second_kernel(scal, other, mine, own, par, out, ordered, p_hi, p_lo):
    @pl.when(pl.program_id(0) == 0)
    def _():
        for block in range(16):
            source = other if block < 8 else mine
            start = block % 8 * 56
            ordered[pl.ds(row_offset(scal, block), 56)] = source[start : start + 56]
        p_hi[...], p_lo[...] = split(ordered[...])

    own_total = dot3(*split(own[...]), p_hi[...], p_lo[...])
    par_total = dot3(*split(par[...]), p_hi[...], p_lo[...])
    lower = lower_lanes((112, 128))
    for pair in range(4):
        cols = slice(pair * 128, pair * 128 + 128)
        a, b = own_total[:, cols], par_total[:, cols]
        out[2 * pair] = jnp.where(lower, a, swap(b))
        out[2 * pair + 1] = jnp.where(lower, swap(a), b)


def second_product(scal, other, mine, own, par):
    half = pl.BlockSpec((448, 512), lambda m, s: (0, 0))
    rows = pl.BlockSpec((112, 896), lambda m, s: ((m + 2 * (1 - s[1])) % 4, 0))
    return pl.pallas_call(
        second_kernel,
        grid_spec=pltpu.PrefetchScalarGridSpec(
            num_scalar_prefetch=1,
            grid=(4,),
            in_specs=[half, half, rows, rows],
            out_specs=pl.BlockSpec((8, 112, 128), lambda m, s: (0, m, 0)),
            scratch_shapes=[pltpu.VMEM((896, 512), F32)] + [pltpu.VMEM((896, 512), BF16)] * 2,
        ),
        out_shape=jax.ShapeDtypeStruct((8, 448, 128), F32),
        compiler_params=pltpu.CompilerParams(vmem_limit_bytes=VMEM_LIMIT),
        cost_estimate=pl.CostEstimate(
            flops=6 * 896 * 896 * 512, bytes_accessed=7 << 20, transcendentals=0
        ),
        name="second_product",
    )(scal, other, mine, own, par)


def last_kernel(scal, iterate, *refs):
    out = refs[-1]
    pieces = refs[:-1]
    x = scal[2]
    rows = pl.ds(pl.multiple_of(scal[1] * 224, 8), 224)
    lower = lower_lanes((224, 128))
    for k in range(4):
        a, b = pieces[k][...], pieces[4 + k][...]
        quarter = (x, 3 - x, x ^ 1, x ^ 2)[k]
        if k in (0, 2):
            value = jnp.where(lower, a, swap(b))
        else:
            value = jnp.where(lower, swap(a), b)
        cols = pl.ds(pl.multiple_of(quarter * 128, 128), 128)
        out[:, cols] = 2.0 * iterate[rows, cols] - value


def last(scal, iterate, pieces):
    piece = pl.BlockSpec((224, 128), lambda i, s: (0, 0))
    mine = pl.BlockSpec((224, 128), lambda i, s: (1, 0))
    return pl.pallas_call(
        last_kernel,
        grid_spec=pltpu.PrefetchScalarGridSpec(
            num_scalar_prefetch=1,
            grid=(1,),
            in_specs=[pl.BlockSpec((448, 512), lambda i, s: (0, 0))] + ([mine] + [piece] * 3) * 2,
            out_specs=pl.BlockSpec((224, 512), lambda i, s: (0, 0)),
        ),
        out_shape=jax.ShapeDtypeStruct((224, 512), F32),
        compiler_params=pltpu.CompilerParams(vmem_limit_bytes=VMEM_LIMIT),
        cost_estimate=pl.CostEstimate(flops=0, bytes_accessed=2 << 20, transcendentals=0),
        name="last",
    )(scal, iterate, *pieces)


def flip(mask):
    return [(r, r ^ mask) for r in range(16)]


def x_mirror():
    pairs = []
    for r in range(16):
        for d in range(2):
            x = 3 - ((r // 2 % 2) * 2 + d)
            pairs.append((r * 2 + d, ((r & 13) | (x // 2) * 2) * 2 + x % 2))
    return pairs


to_core = functools.partial(lax.ppermute, axis_name="row", perm=flip(1))
to_y1 = functools.partial(lax.ppermute, axis_name="row", perm=flip(4))
to_y3 = functools.partial(lax.ppermute, axis_name="row", perm=flip(12))
to_x2 = functools.partial(lax.ppermute, axis_name="row", perm=flip(2))
to_x1 = functools.partial(lax.ppermute, axis_name="depth", perm=[(0, 1), (1, 0)])
to_mirror = functools.partial(lax.ppermute, axis_name=("row", "depth"), perm=x_mirror())


def summed(send, keep):
    got = to_core(send)
    total = keep + got
    first, second = total[:224], total[224:]
    r1, r2 = to_y1(first[:112]), to_y3(second[:112])
    first, second = first[112:] + r1, second[112:] + r2
    s1, s2 = to_y3(first[:56]), to_y1(second[:56])
    first, second = first[56:] + s1, second[56:] + s2
    first = jnp.concatenate([to_y3(first), first], 0)
    second = jnp.concatenate([to_y1(second), second], 0)
    mine = jnp.concatenate([to_y1(first), first, to_y3(second), second], 0)
    return to_core(mine), mine


def local(covariance, iterate):
    row = lax.axis_index("row")
    depth = lax.axis_index("depth")
    y, x = row // 4, (row // 2 % 2) * 2 + depth
    b1, b2 = (y ^ (y // 2)) & 1, y // 2
    scal = jnp.stack([row % 2, depth, x, b1, b2]).astype(jnp.int32)

    window = iterate[:, :SLAB]
    own_w = lax.dynamic_slice_in_dim(window, x * 128, 128, 1)
    par_w = to_mirror(lax.dynamic_slice_in_dim(window, (3 - x) * 128, 128, 1))
    par_cov = to_mirror(covariance)
    par_iter = to_mirror(iterate)
    own_a = transposed(scal, covariance)
    par_a = transposed(scal, par_cov)

    packs = [
        jnp.concatenate([own_w[:, c : c + 64], par_w[:, c : c + 64]], 1) for c in (0, 64)
    ]
    pieces = []
    for pack in packs:
        gathered = lax.all_gather(pack, "col", axis=0)
        other, mine = summed(*first_product(gathered, own_a, par_a))
        result = second_product(scal, other, mine, iterate, par_iter)
        result = lax.psum_scatter(result, "col", scatter_dimension=0)
        away, home = result[:224], result[224:]
        pieces += [result, to_mirror(away), to_x1(away), to_x2(home)]
    return last(scal, iterate, pieces)


def solution(mesh):
    in_specs = (P("row", "col"), P("row", "col"))
    out_specs = P(("row", "depth"), "col")
    return jax.shard_map(local, mesh=mesh, in_specs=in_specs, out_specs=out_specs, check_vma=False)
```

time: 453 us -> 240 us (0.53)
  waiting for transfers between devices: 384 us -> 123 us
  starting transfers between devices: 0.39 us -> 46.4 us
  matrix products: 35 us -> 0 us
  Pallas kernels: 0 us -> 29.1 us
  other arithmetic: 1.91 us -> 6.94 us
    all_gather x4 -> x2, waiting for transfers between devices: 318 us -> 2.85 us  [local(): gathered = lax.all_gather(pack, 'col', axis=0)]
    ppermute x0 -> x29, waiting for transfers between devices: none -> 78.9 us  [the longest x1 28.9 us: local(): par_cov = to_mirror(covariance)]
    ppermute x0 -> x29, starting transfers between devices: none -> 46.3 us  [the longest x6 9.37 us: local(): pieces += [result, to_mirror(away), to_x1(away), to_x2(home)]]
    psum x1 -> x0, waiting for transfers between devices: 42.4 us -> none  [local(): full_product = lax.psum(partial_product, 'depth')]
    dot_general x2 -> x0, matrix products: 35 us -> none  [the longest x1 17.5 us: local(): jnp.dot(lax.all_gather(cov_half, 'col', axis=1, tiled=True), rows_part, p...]
    pallas_call x0 -> x7, Pallas kernels: none -> 29.1 us  [the longest x2 12.8 us: second_product(): pl.pallas_call(second_kernel, grid_spec=pltpu.PrefetchScalarGridSpec(num_...]
    reduce_scatter x1 -> x2, waiting for transfers between devices: 23.6 us -> 41.3 us  [local(): result = lax.psum_scatter(result, 'col', scatter_dimension=0)]
    unnamed x4 -> x46, local copies, waits for them, and re-layouts: 5.75 us -> 15.6 us
  transfers between devices with their start and end apart: 6 -> 33, of which waited for: 6 -> 21; matrix products, arithmetic and copies ran while one was open for 2% -> 5% of each run, Pallas kernels for 0% -> 12%
where the time goes in v1:
time: 240 us; the launch traced here: 239 us
  waiting for transfers between devices  123 us (51%)
  starting transfers between devices  46.4 us (19%)
  Pallas kernels  29.1 us (12%)
  local copies, waits for them, and re-layouts  19.9 us (8%)
  between operations  13.6 us (6%)
  other arithmetic  6.94 us (3%)
    reduce_scatter x2, waiting for transfers between devices, local(): result = lax.psum_scatter(result, 'col', scatter_dimension=0)  41.3 us
    ppermute x1, waiting for transfers between devices, local(): par_cov = to_mirror(covariance)  28.9 us
    ppermute x4, waiting for transfers between devices, summed(): r1, r2 = (to_y1(first[:112]), to_y3(second[:112]))  18 us
    unnamed x46, local copies, waits for them, and re-layouts  15.6 us
    pallas_call x2, Pallas kernels, second_product(): pl.pallas_call(second_kernel, grid_spec=pltpu.PrefetchScalarGridSpec(num_...  12.8 us
    ppermute x4, waiting for transfers between devices, summed(): mine = jnp.concatenate([to_y1(first), first, to_y3(second), second], 0)  12.1 us
    pallas_call x2, Pallas kernels, first_product(): pl.pallas_call(first_kernel, grid=(4,), in_specs=[pl.BlockSpec((8, 448, 1...  11.4 us
    ppermute x6, starting transfers between devices, local(): pieces += [result, to_mirror(away), to_x1(away), to_x2(home)]  9.37 us
  transfers between devices with their start and end apart: 33, of which 21 were waited for; matrix products, arithmetic and copies ran while one was open for 5% of the time, Pallas kernels for 12%

profile of v1, /device:TPU:16, one launch (start us, length us, event | category | flops | bytes accessed | tf_op | source)
XLA Modules:
  0.0 239.0 jit_solution(2256776206678225529)
XLA Ops:
  7.8 2.8 %collective-permute-start = (f32[448,128]{1,0:T(8,128)S(1)}, f32[448,128]{1,0:T(8,128)S(1)}, u32[]{:S(2)}, u32[]{:S(2)}) collective-permute-start(f32[448,128]{1,0:T(8,128)S(1)} %constant_dynamic-slice_fusion.1), channel_id=1, source_target_pairs={{0,33},{1,32},{16,49},{17,48},{32,1},{33,0},{48,17},{49,16},{64,97... | collective-permute-start | bytes 688136 | tf_op jit(solution)/shard_map/ppermute | solution.py:235
  11.5 4.9 %collective-permute-done = f32[448,128]{1,0:T(8,128)S(1)} collective-permute-done((f32[448,128]{1,0:T(8,128)S(1)}, f32[448,128]{1,0:T(8,128)S(1)}, u32[]{:S(2)}, u32[]{:S(2)}) %collective-permute-start) | collective-permute-done | bytes 229408 | tf_op jit(solution)/shard_map/ppermute | solution.py:235
  17.5 2.8 %collective-permute-start.1 = (f32[448,896]{1,0:T(8,128)S(1)}, f32[448,896]{1,0:T(8,128)S(1)}, u32[]{:S(2)}, u32[]{:S(2)}) collective-permute-start(f32[448,896]{1,0:T(8,128)S(1)} %copy-done.1), channel_id=1, source_target_pairs={{0,33},{1,32},{16,49},{17,48},{32,1},{33,0},{48,17},{49,16},{64,97... | collective-permute-start | bytes 4816904 | tf_op jit(solution)/shard_map/ppermute | solution.py:236
  25.9 28.9 %collective-permute-done.1.tile = f32[448,896]{1,0:T(8,128)S(1)} collective-permute-done((f32[448,896]{1,0:T(8,128)S(1)}, f32[448,896]{1,0:T(8,128)S(1)}, u32[]{:S(2)}, u32[]{:S(2)}) %collective-permute-start.1) | collective-permute-done | bytes 1605664 | tf_op jit(solution)/shard_map/ppermute | solution.py:236
  57.4 2.8 %all-gather.7.cloned.1.call-done = f32[3584,128]{1,0:T(8,128)} async-done(((f32[448,128]{1,0:T(8,128)}), f32[3584,128]{1,0:T(8,128)}) %all-gather.7.cloned.1.call-update) | async-done | bytes 1835024 | tf_op jit(solution)/shard_map/all_gather | solution.py:246
  63.8 5.7 %first_product.3 = (f32[448,512]{1,0:T(8,128)S(1)}, f32[448,512]{1,0:T(8,128)S(1)}) custom-call(f32[8,448,128]{2,1,0:T(8,128)} %bitcast.20, bf16[896,448]{1,0:T(8,128)(2,1)S(1)} %copy-done.5, bf16[896,448]{1,0:T(8,128)(2,1)S(1)} %copy-done.8, bf16[896,448]{1,0:T(8,128)(2,1)S(1)} %get-tuple-element.15.par_hi, bf16[896,448]{1,0:T(8,128)(2,1)S(1)} %copy-done.13), custom_call_target="tpu_custom_call" | custom-call | flops 2466250752 | bytes 7340032 | tf_op jit(solution)/shard_map/first_product/pallas_call | solution.py:98
  72.9 7.1 %collective-permute-done.21 = f32[112,512]{1,0:T(8,128)S(1)} collective-permute-done((f32[112,512]{1,0:T(8,128)S(1)}, f32[112,512]{1,0:T(8,128)S(1)}, u32[]{:S(2)}, u32[]{:S(2)}) %collective-permute-start.21) | collective-permute-done | bytes 229408 | tf_op jit(solution)/shard_map/ppermute | solution.py:216
  80.1 2.5 %collective-permute-start.17 = (f32[112,512]{1,0:T(8,128)S(1)}, f32[112,512]{1,0:T(8,128)S(1)}, u32[]{:S(2)}, u32[]{:S(2)}) collective-permute-start(f32[112,512]{1,0:T(8,128)S(1)} %get-tuple-element.22), channel_id=1, source_target_pairs={{0,64},{16,80},{32,96},{48,112},{64,0},{80,16},{96,32},{112,48},{1... | collective-permute-start | bytes 688136 | tf_op jit(solution)/shard_map/ppermute | solution.py:216
  82.6 5.2 %collective-permute-done.17 = f32[112,512]{1,0:T(8,128)S(1)} collective-permute-done((f32[112,512]{1,0:T(8,128)S(1)}, f32[112,512]{1,0:T(8,128)S(1)}, u32[]{:S(2)}, u32[]{:S(2)}) %collective-permute-start.17) | collective-permute-done | bytes 229408 | tf_op jit(solution)/shard_map/ppermute | solution.py:216
  87.9 2.8 %collective-permute-start.12 = (f32[448,896]{1,0:T(8,128)S(1)}, f32[448,896]{1,0:T(8,128)S(1)}, u32[]{:S(2)}, u32[]{:S(2)}) collective-permute-start(f32[448,896]{1,0:T(8,128)S(1)} %copy-done), channel_id=1, source_target_pairs={{0,33},{1,32},{16,49},{17,48},{32,1},{33,0},{48,17},{49,16},{64,97... | collective-permute-start | bytes 4816904 | tf_op jit(solution)/shard_map/ppermute | solution.py:237
  99.3 3.8 %collective-permute-start.20 = (f32[112,512]{1,0:T(8,128)}, f32[112,512]{1,0:T(8,128)}, u32[]{:S(2)}, u32[]{:S(2)}) collective-permute-start(f32[112,512]{1,0:T(8,128)} %pad_maximum_fusion.4), channel_id=1, source_target_pairs={{0,64},{16,80},{32,96},{48,112},{64,0},{80,16},{96,32},{112,48},{1... | collective-permute-start | bytes 688136 | tf_op jit(solution)/shard_map/ppermute | solution.py:222
  107.8 5.7 %first_product.2 = (f32[448,512]{1,0:T(8,128)S(1)}, f32[448,512]{1,0:T(8,128)S(1)}) custom-call(f32[8,448,128]{2,1,0:T(8,128)} %bitcast.19, bf16[896,448]{1,0:T(8,128)(2,1)S(1)} %copy-done.6, bf16[896,448]{1,0:T(8,128)(2,1)S(1)} %copy-done.9, bf16[896,448]{1,0:T(8,128)(2,1)S(1)} %copy-done.11, bf16[896,448]{1,0:T(8,128)(2,1)S(1)} %copy-done.14), custom_call_target="tpu_custom_call" | custom-call | flops 2466250752 | bytes 7340032 | tf_op jit(solution)/shard_map/first_product/pallas_call | solution.py:98
  115.8 7.0 %collective-permute-done.24 = f32[112,512]{1,0:T(8,128)S(1)} collective-permute-done((f32[112,512]{1,0:T(8,128)S(1)}, f32[112,512]{1,0:T(8,128)S(1)}, u32[]{:S(2)}, u32[]{:S(2)}) %collective-permute-start.24) | collective-permute-done | bytes 229408 | tf_op jit(solution)/shard_map/ppermute | solution.py:222
  126.3 6.4 %second_product.3 = f32[8,448,128]{2,1,0:T(8,128)} custom-call(s32[5]{0:T(128)S(1)} %stack.23.scal, f32[448,512]{1,0:T(8,128)S(1)} %collective-permute-done.25.other, f32[448,512]{1,0:T(8,128)S(1)} %constant_dynamic-update-slice_fusion.6.mine, f32[448,896]{1,0:T(8,128)S(1)} %copy-done, f32[448,896]{1,0:T(8,128)S(1)} %collective-permute-done.12.par), custom_call_target="tpu_custom_call" | custom-call | flops 2466250752 | bytes 7340032 | tf_op jit(solution)/shard_map/second_product/pallas_call | solution.py:138
  136.0 5.8 %collective-permute-done.3 = f32[112,512]{1,0:T(8,128)S(1)} collective-permute-done((f32[112,512]{1,0:T(8,128)S(1)}, f32[112,512]{1,0:T(8,128)S(1)}, u32[]{:S(2)}, u32[]{:S(2)}) %collective-permute-start.3) | collective-permute-done | bytes 229408 | tf_op jit(solution)/shard_map/ppermute | solution.py:216
  148.6 3.3 %collective-permute-start.9 = (f32[56,512]{1,0:T(8,128)S(1)}, f32[56,512]{1,0:T(8,128)S(1)}, u32[]{:S(2)}, u32[]{:S(2)}) collective-permute-start(f32[56,512]{1,0:T(8,128)S(1)} %slice_add_fusion.6), channel_id=1, source_target_pairs={{0,64},{16,80},{32,96},{48,112},{64,0},{80,16},{96,32},{112,48},{1... | collective-permute-start | bytes 344072 | tf_op jit(solution)/shard_map/ppermute | solution.py:221
  152.5 4.0 %collective-permute-start.6 = (f32[112,512]{1,0:T(8,128)S(1)}, f32[112,512]{1,0:T(8,128)S(1)}, u32[]{:S(2)}, u32[]{:S(2)}) collective-permute-start(f32[112,512]{1,0:T(8,128)S(1)} %pad_maximum_fusion.1), channel_id=1, source_target_pairs={{0,64},{16,80},{32,96},{48,112},{64,0},{80,16},{96,32},{112,48},{1... | collective-permute-start | bytes 688136 | tf_op jit(solution)/shard_map/ppermute | solution.py:222
  157.4 3.1 %collective-permute-done.6 = f32[112,512]{1,0:T(8,128)S(1)} collective-permute-done((f32[112,512]{1,0:T(8,128)S(1)}, f32[112,512]{1,0:T(8,128)S(1)}, u32[]{:S(2)}, u32[]{:S(2)}) %collective-permute-start.6) | collective-permute-done | bytes 229408 | tf_op jit(solution)/shard_map/ppermute | solution.py:222
  162.8 2.5 %collective-permute-done.11.other = f32[448,512]{1,0:T(8,128)S(1)} collective-permute-done((f32[448,512]{1,0:T(8,128)S(1)}, f32[448,512]{1,0:T(8,128)S(1)}, u32[]{:S(2)}, u32[]{:S(2)}) %collective-permute-start.11) | collective-permute-done | bytes 917536 | tf_op jit(solution)/shard_map/ppermute | solution.py:223
  165.3 6.4 %second_product.2 = f32[8,448,128]{2,1,0:T(8,128)} custom-call(s32[5]{0:T(128)S(1)} %stack.23.scal, f32[448,512]{1,0:T(8,128)S(1)} %collective-permute-done.11.other, f32[448,512]{1,0:T(8,128)S(1)} %constant_dynamic-update-slice_fusion.mine, f32[448,896]{1,0:T(8,128)S(1)} %copy-done, f32[448,896]{1,0:T(8,128)S(1)} %collective-permute-done.12.par), custom_call_target="tpu_custom_call" | custom-call | flops 2466250752 | bytes 7340032 | tf_op jit(solution)/shard_map/second_product/pallas_call | solution.py:138
  175.1 2.7 %collective-permute-start.26 = (f32[224,128]{1,0:T(8,128)S(1)}, f32[224,128]{1,0:T(8,128)S(1)}, u32[]{:S(2)}, u32[]{:S(2)}) collective-permute-start(f32[224,128]{1,0:T(8,128)S(1)} %get-tuple-element.28), channel_id=1, source_target_pairs={{0,33},{1,32},{16,49},{17,48},{32,1},{33,0},{48,17},{49,16},{64,97... | collective-permute-start | bytes 344072 | tf_op jit(solution)/shard_map/ppermute | solution.py:251
  178.2 38.8 %reduce-scatter.3.cloned.1.call-done = f32[1,448,128]{2,1,0:T(8,128)} async-done(((f32[8,448,128]{2,1,0:T(8,128)}), f32[1,448,128]{2,1,0:T(8,128)}) %reduce-scatter.3.cloned.1.call-update) | async-done | bytes 229392 | tf_op jit(solution)/shard_map/reduce_scatter | solution.py:249
  218.0 2.5 %collective-permute-start.13 = (f32[224,128]{1,0:T(8,128)S(1)}, f32[224,128]{1,0:T(8,128)S(1)}, u32[]{:S(2)}, u32[]{:S(2)}) collective-permute-start(f32[224,128]{1,0:T(8,128)S(1)} %get-tuple-element.32), channel_id=1, source_target_pairs={{0,33},{1,32},{16,49},{17,48},{32,1},{33,0},{48,17},{49,16},{64,97... | collective-permute-start | bytes 344072 | tf_op jit(solution)/shard_map/ppermute | solution.py:251
  224.3 2.8 %collective-permute-done.28.refs_7_ = f32[224,128]{1,0:T(8,128)S(1)} collective-permute-done((f32[224,128]{1,0:T(8,128)S(1)}, f32[224,128]{1,0:T(8,128)S(1)}, u32[]{:S(2)}, u32[]{:S(2)}) %collective-permute-start.28) | collective-permute-done | bytes 114720 | tf_op jit(solution)/shard_map/ppermute | solution.py:251
  (130 shorter events, 65.1 us)
Async XLA Ops:
  6.5 53.7 %all-gather.7.cloned.1.call-start = ((), (), s32[]{:S(2)}) async-start(), calls=%async_computation.5 | async-start | bytes 2064384 | tf_op jit(solution)/shard_map/all_gather | solution.py:246
  7.8 8.6 %collective-permute-start = (f32[448,128]{1,0:T(8,128)S(1)}, f32[448,128]{1,0:T(8,128)S(1)}, u32[]{:S(2)}, u32[]{:S(2)}) collective-permute-start(f32[448,128]{1,0:T(8,128)S(1)} %constant_dynamic-slice_fusion.1), channel_id=1, source_target_pairs={{0,33},{1,32},{16,49},{17,48},{32,1},{33,0},{48,17},{49,16},{64,97... | collective-permute-start | bytes 688136 | tf_op jit(solution)/shard_map/ppermute | solution.py:235
  17.5 85.6 %all-gather.5.cloned.1.call-start = ((), (), s32[]{:S(2)}) async-start(), calls=%async_computation.4 | async-start | bytes 2064384 | tf_op jit(solution)/shard_map/all_gather | solution.py:246
  17.5 37.3 %collective-permute-start.1 = (f32[448,896]{1,0:T(8,128)S(1)}, f32[448,896]{1,0:T(8,128)S(1)}, u32[]{:S(2)}, u32[]{:S(2)}) collective-permute-start(f32[448,896]{1,0:T(8,128)S(1)} %copy-done.1), channel_id=1, source_target_pairs={{0,33},{1,32},{16,49},{17,48},{32,1},{33,0},{48,17},{49,16},{64,97... | collective-permute-start | bytes 4816904 | tf_op jit(solution)/shard_map/ppermute | solution.py:236
  22.2 152.0 %reduce-scatter.5.cloned.1.call-start = ((), (), s32[]{:S(2)}) async-start(), calls=%async_computation.3 | async-start | bytes 2064384 | tf_op jit(solution)/shard_map/reduce_scatter | solution.py:249
  72.3 7.7 %collective-permute-start.21 = (f32[112,512]{1,0:T(8,128)S(1)}, f32[112,512]{1,0:T(8,128)S(1)}, u32[]{:S(2)}, u32[]{:S(2)}) collective-permute-start(f32[112,512]{1,0:T(8,128)S(1)} %slice.145), channel_id=1, source_target_pairs={{0,192},{16,208},{32,224},{48,240},{64,128},{80,144},{96,160},{112... | collective-permute-start | bytes 688136 | tf_op jit(solution)/shard_map/ppermute | solution.py:216
  80.1 7.7 %collective-permute-start.17 = (f32[112,512]{1,0:T(8,128)S(1)}, f32[112,512]{1,0:T(8,128)S(1)}, u32[]{:S(2)}, u32[]{:S(2)}) collective-permute-start(f32[112,512]{1,0:T(8,128)S(1)} %get-tuple-element.22), channel_id=1, source_target_pairs={{0,64},{16,80},{32,96},{48,112},{64,0},{80,16},{96,32},{112,48},{1... | collective-permute-start | bytes 688136 | tf_op jit(solution)/shard_map/ppermute | solution.py:216
  87.9 37.1 %collective-permute-start.12 = (f32[448,896]{1,0:T(8,128)S(1)}, f32[448,896]{1,0:T(8,128)S(1)}, u32[]{:S(2)}, u32[]{:S(2)}) collective-permute-start(f32[448,896]{1,0:T(8,128)S(1)} %copy-done), channel_id=1, source_target_pairs={{0,33},{1,32},{16,49},{17,48},{32,1},{33,0},{48,17},{49,16},{64,97... | collective-permute-start | bytes 4816904 | tf_op jit(solution)/shard_map/ppermute | solution.py:237
  95.7 17.9 %collective-permute-start.23 = (f32[56,512]{1,0:T(8,128)S(1)}, f32[56,512]{1,0:T(8,128)}, u32[]{:S(2)}, u32[]{:S(2)}) collective-permute-start(f32[56,512]{1,0:T(8,128)S(1)} %slice_add_fusion.4), channel_id=1, source_target_pairs={{0,64},{16,80},{32,96},{48,112},{64,0},{80,16},{96,32},{112,48},{1... | collective-permute-start | bytes 344072 | tf_op jit(solution)/shard_map/ppermute | solution.py:221
  99.3 15.6 %collective-permute-start.20 = (f32[112,512]{1,0:T(8,128)}, f32[112,512]{1,0:T(8,128)}, u32[]{:S(2)}, u32[]{:S(2)}) collective-permute-start(f32[112,512]{1,0:T(8,128)} %pad_maximum_fusion.4), channel_id=1, source_target_pairs={{0,64},{16,80},{32,96},{48,112},{64,0},{80,16},{96,32},{112,48},{1... | collective-permute-start | bytes 688136 | tf_op jit(solution)/shard_map/ppermute | solution.py:222
  113.5 10.3 %collective-permute-start.2 = (f32[448,512]{1,0:T(8,128)S(1)}, f32[448,512]{1,0:T(8,128)S(1)}, u32[]{:S(2)}, u32[]{:S(2)}) collective-permute-start(f32[448,512]{1,0:T(8,128)S(1)} %get-tuple-element.18), channel_id=1, source_target_pairs={{0,16},{16,0},{32,48},{48,32},{64,80},{80,64},{96,112},{112,96},{1... | collective-permute-start | bytes 2752520 | tf_op jit(solution)/shard_map/ppermute | solution.py:213
  114.5 8.3 %collective-permute-start.24 = (f32[112,512]{1,0:T(8,128)S(1)}, f32[112,512]{1,0:T(8,128)S(1)}, u32[]{:S(2)}, u32[]{:S(2)}) collective-permute-start(f32[112,512]{1,0:T(8,128)S(1)} %pad_maximum_fusion.5), channel_id=1, source_target_pairs={{0,192},{16,208},{32,224},{48,240},{64,128},{80,144},{96,160},{112... | collective-permute-start | bytes 688136 | tf_op jit(solution)/shard_map/ppermute | solution.py:222
  124.1 8.7 %collective-permute-start.7 = (f32[112,512]{1,0:T(8,128)S(1)}, f32[112,512]{1,0:T(8,128)}, u32[]{:S(2)}, u32[]{:S(2)}) collective-permute-start(f32[112,512]{1,0:T(8,128)S(1)} %slice.134), channel_id=1, source_target_pairs={{0,192},{16,208},{32,224},{48,240},{64,128},{80,144},{96,160},{112... | collective-permute-start | bytes 688136 | tf_op jit(solution)/shard_map/ppermute | solution.py:216
  132.7 84.3 %reduce-scatter.3.cloned.1.call-start = ((), (), s32[]{:S(2)}) async-start(), calls=%async_computation.2 | async-start | bytes 2064384 | tf_op jit(solution)/shard_map/reduce_scatter | solution.py:249
  134.0 7.7 %collective-permute-start.3 = (f32[112,512]{1,0:T(8,128)S(1)}, f32[112,512]{1,0:T(8,128)S(1)}, u32[]{:S(2)}, u32[]{:S(2)}) collective-permute-start(f32[112,512]{1,0:T(8,128)S(1)} %get-tuple-element.26), channel_id=1, source_target_pairs={{0,64},{16,80},{32,96},{48,112},{64,0},{80,16},{96,32},{112,48},{1... | collective-permute-start | bytes 688136 | tf_op jit(solution)/shard_map/ppermute | solution.py:216
  148.6 7.9 %collective-permute-start.9 = (f32[56,512]{1,0:T(8,128)S(1)}, f32[56,512]{1,0:T(8,128)S(1)}, u32[]{:S(2)}, u32[]{:S(2)}) collective-permute-start(f32[56,512]{1,0:T(8,128)S(1)} %slice_add_fusion.6), channel_id=1, source_target_pairs={{0,64},{16,80},{32,96},{48,112},{64,0},{80,16},{96,32},{112,48},{1... | collective-permute-start | bytes 344072 | tf_op jit(solution)/shard_map/ppermute | solution.py:221
  152.5 8.0 %collective-permute-start.6 = (f32[112,512]{1,0:T(8,128)S(1)}, f32[112,512]{1,0:T(8,128)S(1)}, u32[]{:S(2)}, u32[]{:S(2)}) collective-permute-start(f32[112,512]{1,0:T(8,128)S(1)} %pad_maximum_fusion.1), channel_id=1, source_target_pairs={{0,64},{16,80},{32,96},{48,112},{64,0},{80,16},{96,32},{112,48},{1... | collective-permute-start | bytes 688136 | tf_op jit(solution)/shard_map/ppermute | solution.py:222
  156.5 6.1 %collective-permute-start.10 = (f32[112,512]{1,0:T(8,128)S(1)}, f32[112,512]{1,0:T(8,128)S(1)}, u32[]{:S(2)}, u32[]{:S(2)}) collective-permute-start(f32[112,512]{1,0:T(8,128)S(1)} %pad_maximum_fusion.2), channel_id=1, source_target_pairs={{0,192},{16,208},{32,224},{48,240},{64,128},{80,144},{96,160},{112... | collective-permute-start | bytes 688136 | tf_op jit(solution)/shard_map/ppermute | solution.py:222
  175.1 47.7 %collective-permute-start.26 = (f32[224,128]{1,0:T(8,128)S(1)}, f32[224,128]{1,0:T(8,128)S(1)}, u32[]{:S(2)}, u32[]{:S(2)}) collective-permute-start(f32[224,128]{1,0:T(8,128)S(1)} %get-tuple-element.28), channel_id=1, source_target_pairs={{0,33},{1,32},{16,49},{17,48},{32,1},{33,0},{48,17},{49,16},{64,97... | collective-permute-start | bytes 344072 | tf_op jit(solution)/shard_map/ppermute | solution.py:251
  177.8 46.4 %collective-permute-start.27 = (f32[224,128]{1,0:T(8,128)S(1)}, f32[224,128]{1,0:T(8,128)S(1)}, u32[]{:S(2)}, u32[]{:S(2)}) collective-permute-start(f32[224,128]{1,0:T(8,128)S(1)} %get-tuple-element.28), channel_id=1, source_target_pairs={{0,1},{1,0},{2,3},{3,2},{4,5},{5,4},{6,7},{7,6},{8,9},{9,8},{10,11... | collective-permute-start | bytes 344072 | tf_op jit(solution)/shard_map/ppermute | solution.py:251
  218.0 9.0 %collective-permute-start.13 = (f32[224,128]{1,0:T(8,128)S(1)}, f32[224,128]{1,0:T(8,128)S(1)}, u32[]{:S(2)}, u32[]{:S(2)}) collective-permute-start(f32[224,128]{1,0:T(8,128)S(1)} %get-tuple-element.32), channel_id=1, source_target_pairs={{0,33},{1,32},{16,49},{17,48},{32,1},{33,0},{48,17},{49,16},{64,97... | collective-permute-start | bytes 344072 | tf_op jit(solution)/shard_map/ppermute | solution.py:251
  220.5 6.5 %collective-permute-start.14 = (f32[224,128]{1,0:T(8,128)S(1)}, f32[224,128]{1,0:T(8,128)S(1)}, u32[]{:S(2)}, u32[]{:S(2)}) collective-permute-start(f32[224,128]{1,0:T(8,128)S(1)} %get-tuple-element.32), channel_id=1, source_target_pairs={{0,1},{1,0},{2,3},{3,2},{4,5},{5,4},{6,7},{7,6},{8,9},{9,8},{10,11... | collective-permute-start | bytes 344072 | tf_op jit(solution)/shard_map/ppermute | solution.py:251
  220.7 6.3 %collective-permute-start.28 = (f32[224,128]{1,0:T(8,128)S(1)}, f32[224,128]{1,0:T(8,128)S(1)}, u32[]{:S(2)}, u32[]{:S(2)}) collective-permute-start(f32[224,128]{1,0:T(8,128)S(1)} %get-tuple-element.27), channel_id=1, source_target_pairs={{0,32},{16,48},{32,0},{48,16},{64,96},{80,112},{96,64},{112,80},{1... | collective-permute-start | bytes 344072 | tf_op jit(solution)/shard_map/ppermute | solution.py:251
  222.8 6.3 %collective-permute-start.15 = (f32[224,128]{1,0:T(8,128)S(1)}, f32[224,128]{1,0:T(8,128)S(1)}, u32[]{:S(2)}, u32[]{:S(2)}) collective-permute-start(f32[224,128]{1,0:T(8,128)S(1)} %get-tuple-element.31), channel_id=1, source_target_pairs={{0,32},{16,48},{32,0},{48,16},{64,96},{80,112},{96,64},{112,80},{1... | collective-permute-start | bytes 344072 | tf_op jit(solution)/shard_map/ppermute | solution.py:251
  (27 other events, 99.1 us)
Sparse Core Ops, SparseCore 0:
  17.6 42.6 all-gather.6
  62.1 39.1 all-gather.4
  132.9 41.2 reduce-scatter.4
  176.6 40.4 reduce-scatter.2
